TPU v7x, 512 devices: a whole 4x8x8 slice. The times are simulated.
512 devices in a mesh: bucket: 128 (over x, y, z_lo, core), rep: 4 (over z_hi).
Axes of the slice: x: 4, y: 8, z: 8 (z_hi: 4, z_lo: 2; z = z_hi * 2 + z_lo), core: 2. Of those that a mesh axis runs over, the one named last changes fastest.
Arguments:
- src_table: float32 [262144, 256], P(('bucket', 'rep')), may hold values from -6 to 6
- src_state: float32 [262144], P(('bucket', 'rep')), may hold values from 0.05 to 0.5
- dst_table: float32 [65536, 256], P(('bucket', 'rep')), may hold values from -6 to 6
- dst_state: float32 [65536], P(('bucket', 'rep')), may hold values from 0.05 to 0.5
- rel_table: float32 [64, 256], replicated, may hold values from 0.25 to 1.75
- partners: int32 [2, 128], replicated, may hold values from 0 to 127, as said below
- tiles: int32 [128, 4, 2, 64], P('bucket', 'rep'), may hold values from 0 to 15
- tile_rel: int32 [128, 4, 2, 64], P('bucket', 'rep'), may hold values from 0 to 63
- counts: int32 [128, 4, 2], P('bucket', 'rep'), may hold values from 1 to 64, as said below
Outputs:
- src_out: float32 [262144, 256], P(('bucket', 'rep'))
- src_state_out: float32 [262144], P(('bucket', 'rep'))
- dst_out: float32 [65536, 256], P(('bucket', 'rep'))
- dst_state_out: float32 [65536], P(('bucket', 'rep'))
Inputs may be any that keep to these rules, and one draw needn't show every extreme that they name: partners[k, b] = b XOR m_k for one mask m_k of round k, 1 to 127, a different mask in each round. Only the first counts[b, r, k] slots of a device's round are live; some device holds 64 live tiles in every draw.
All inputs are finite; a program needn't handle non-finite values.
Results may differ from a plain program's by a relative error of at most 0.002.
Values may be sent and summed in bfloat16 or wider, within the bound.
A program may use at most 64 MiB of HBM per device.

v0:
```python
import functools

import jax
import jax.numpy as jnp
from jax import lax
from jax.experimental import pallas as pl
from jax.experimental.pallas import tpu as pltpu
from jax.sharding import PartitionSpec as P

D = 256
TILE = 128
ROUNDS = 2


learn_rate = 0.1


HALF = TILE // 2
MESH = pl.DeviceIdType.MESH


def paired(mask):
    me = lax.axis_index("bucket")
    other = me
    for bit in range(mask.bit_length()):
        if mask >> bit & 1:
            other = other + (1 << bit) * (1 - 2 * lax.rem(lax.div(me, 1 << bit), 2))
    return other


def around():
    me = lax.axis_index("rep")
    return me, lax.rem(me + 3, 4), lax.rem(me + 1, 4), lax.rem(me + 2, 4)


def greet(devices):
    barrier = pltpu.get_barrier_semaphore()
    for device in devices:
        pl.semaphore_signal(barrier, inc=1, device_id=device, device_id_type=MESH)
    pl.semaphore_wait(barrier, len(devices))


def rows(quarter, half):
    return pl.ds(pl.multiple_of(quarter * TILE + half * HALF, HALF), HALF)


def gather_kernel(mask, low_ref, part_ref, send, recv):
    me, left, right, far = around()
    to_left, to_right, to_pair = {"rep": left}, {"rep": right}, {"bucket": paired(mask)}

    def copy(slot, src, dst, device):
        return pltpu.make_async_remote_copy(
            src, dst, send.at[slot], recv.at[slot], device_id=device, device_id_type=MESH
        )

    greet((to_pair, to_left, to_right) if mask else (to_left, to_right))
    own = [part_ref.at[rows(me, half)] for half in range(2)]
    if mask:
        hop = [copy(half, low_ref.at[rows(0, half)], own[half], to_pair) for half in range(2)]
        hop[0].start()
        hop[1].start()
    else:
        part_ref[pl.ds(pl.multiple_of(me * TILE, TILE), TILE), :] = low_ref[...]
        hop = []
    going_right = [copy(2 + half, own[half], own[half], to_right) for half in range(2)]
    going_left = [copy(4 + half, own[half], own[half], to_left) for half in range(2)]
    if mask:
        hop[0].wait_recv()
    going_right[0].start()
    going_left[0].start()
    if mask:
        hop[1].wait_recv()
    going_left[1].start()
    going_right[1].start()
    passed = part_ref.at[rows(left, 0)]
    on_right = copy(6, passed, passed, to_right)
    going_right[0].wait_recv()
    on_right.start()
    passed = part_ref.at[rows(right, 1)]
    on_left = copy(7, passed, passed, to_left)
    going_left[1].wait_recv()
    on_left.start()
    going_left[0].wait_recv()
    going_right[1].wait_recv()
    on_right.wait_recv()
    on_left.wait_recv()
    for sent in (*hop, *going_right, *going_left, on_right, on_left):
        sent.wait_send()


def gathered(mask, collective_id, low):
    vmem = pl.BlockSpec(memory_space=pltpu.VMEM)
    return pl.pallas_call(
        functools.partial(gather_kernel, mask),
        out_shape=jax.ShapeDtypeStruct((4 * TILE, D), jnp.bfloat16),
        in_specs=[vmem],
        out_specs=vmem,
        scratch_shapes=[pltpu.SemaphoreType.DMA((8,)), pltpu.SemaphoreType.DMA((8,))],
        compiler_params=pltpu.CompilerParams(
            collective_id=collective_id, has_side_effects=True, vmem_limit_bytes=16 * 2**20
        ),
    )(low)


def diagonal():
    row = lax.broadcasted_iota(jnp.int32, (TILE, TILE), 0)
    col = lax.broadcasted_iota(jnp.int32, (TILE, TILE), 1)
    return row == col


def adagrad_block(table, state_row, grad, diag):
    mean = jnp.sum(grad * grad, axis=1, keepdims=True) * (1 / D)
    state = jnp.sum(jnp.where(diag, state_row, 0.0), axis=1, keepdims=True) + mean
    table = table - grad * (learn_rate / jnp.sqrt(state))
    return table, jnp.sum(jnp.where(diag, state, 0.0), axis=0, keepdims=True)


def reduce_kernel(
    mask, part_ref, got, relay, added, side, total, send, recv
):
    me, left, right, far = around()
    to_left, to_right, to_pair = {"rep": left}, {"rep": right}, {"bucket": paired(mask)}

    def copy(slot, src, dst, device):
        return pltpu.make_async_remote_copy(
            src, dst, send.at[slot], recv.at[slot], device_id=device, device_id_type=MESH
        )

    def wide(ref):
        return ref[...].astype(jnp.float32)

    greet((to_pair, to_left, to_right) if mask else (to_left, to_right))
    first = copy(0, part_ref.at[rows(far, 0)], relay.at[rows(0, 0)], to_left)
    second = copy(1, part_ref.at[rows(far, 1)], relay.at[rows(0, 1)], to_right)
    left_one = copy(2, part_ref.at[rows(left, 1)], side.at[rows(1, 1)], to_left)
    right_zero = copy(3, part_ref.at[rows(right, 0)], side.at[rows(0, 0)], to_right)
    left_zero = copy(4, added.at[rows(0, 0)], side.at[rows(1, 0)], to_left)
    right_one = copy(5, added.at[rows(0, 1)], side.at[rows(0, 1)], to_right)
    if mask:
        back = [copy(6 + half, total.at[rows(0, half)], got.at[rows(0, half)], to_pair) for half in range(2)]
    else:
        back, total = [], got
    first.start()
    second.start()
    left_one.start()
    right_zero.start()
    first.wait_recv()
    added[rows(0, 0), :] = (
        wide(relay.at[rows(0, 0)]) + wide(part_ref.at[rows(left, 0)])
    ).astype(jnp.bfloat16)
    left_zero.start()
    second.wait_recv()
    added[rows(0, 1), :] = (
        wide(relay.at[rows(0, 1)]) + wide(part_ref.at[rows(right, 1)])
    ).astype(jnp.bfloat16)
    right_one.start()
    for half, needed in ((0, (right_zero, left_zero)), (1, (left_one, right_one))):
        needed[0].wait_recv()
        needed[1].wait_recv()
        total[rows(0, half), :] = (
            wide(part_ref.at[rows(me, half)])
            + wide(side.at[rows(0, half)])
            + wide(side.at[rows(1, half)])
        ).astype(jnp.bfloat16)
        if mask:
            back[half].start()
    for sent in back:
        sent.wait_recv()
    for sent in (first, second, left_one, right_zero, left_zero, right_one, *back):
        sent.wait_send()


def reduced(mask, collective_id, dst_part):
    vmem = pl.BlockSpec(memory_space=pltpu.VMEM)
    low = jnp.bfloat16
    return pl.pallas_call(
        functools.partial(reduce_kernel, mask),
        out_shape=jax.ShapeDtypeStruct((TILE, D), low),
        in_specs=[vmem],
        out_specs=vmem,
        scratch_shapes=[
            pltpu.VMEM((TILE, D), low),
            pltpu.VMEM((TILE, D), low),
            pltpu.VMEM((2 * TILE, D), low),
            pltpu.VMEM((TILE, D), low),
            pltpu.SemaphoreType.DMA((8,)),
            pltpu.SemaphoreType.DMA((8,)),
        ],
        compiler_params=pltpu.CompilerParams(
            collective_id=collective_id, has_side_effects=True, vmem_limit_bytes=16 * 2**20
        ),
    )(dst_part)


def permute_kernel(mask, rows_ref, moved_ref, send, recv):
    to_pair = {"bucket": paired(mask)}
    greet((to_pair,))
    copy = pltpu.make_async_remote_copy(
        rows_ref, moved_ref, send, recv, device_id=to_pair, device_id_type=MESH
    )
    copy.start()
    copy.wait()


def permuted(mask, collective_id, block):
    if not mask:
        return block
    vmem = pl.BlockSpec(memory_space=pltpu.VMEM)
    return pl.pallas_call(
        functools.partial(permute_kernel, mask),
        out_shape=jax.ShapeDtypeStruct(block.shape, block.dtype),
        in_specs=[vmem],
        out_specs=vmem,
        scratch_shapes=[pltpu.SemaphoreType.DMA, pltpu.SemaphoreType.DMA],
        compiler_params=pltpu.CompilerParams(
            collective_id=collective_id, has_side_effects=True, vmem_limit_bytes=16 * 2**20
        ),
    )(block)


def adagrad_kernel(table_ref, state_ref, grad_ref, table_out, state_out, low_out):
    table_out[...], state_out[...] = adagrad_block(
        table_ref[...], state_ref[...], grad_ref[...].astype(jnp.float32), diagonal()
    )
    low_out[...] = table_out[...].astype(jnp.bfloat16)


def updated(table, state, grad):
    vmem = pl.BlockSpec(memory_space=pltpu.VMEM)
    return pl.pallas_call(
        adagrad_kernel,
        out_shape=(
            jax.ShapeDtypeStruct(table.shape, jnp.float32),
            jax.ShapeDtypeStruct(state.shape, jnp.float32),
            jax.ShapeDtypeStruct(grad.shape, jnp.bfloat16),
        ),
        in_specs=[vmem] * 3,
        out_specs=(vmem,) * 3,
        compiler_params=pltpu.CompilerParams(vmem_limit_bytes=16 * 2**20),
    )(table, state, grad)


Y_MASKS = tuple(y << 2 for y in range(8))
OTHER_MASKS = tuple((x << 5) + low for x in range(4) for low in range(4))


def along_y(make, first_id, round_mask, block):
    branches = [functools.partial(make, mask, first_id + i) for i, mask in enumerate(Y_MASKS)]
    return lax.switch((round_mask >> 2) & 7, branches, block)


def along_others(first_id, round_mask, block):
    branches = [
        functools.partial(permuted, mask, first_id + i) for i, mask in enumerate(OTHER_MASKS)
    ]
    return lax.switch((round_mask >> 5) * 4 + (round_mask & 3), branches, block)


UNROLL = 4


def tile_kernel(round_index, code_ref, rel_id_ref, count_ref, src_ref, part_ref, rel_ref, state_ref,
    table_out, state_out, dst_out, src_low, src_grad, dst_grad
):
    src_low[...] = src_ref[...].astype(jnp.bfloat16).astype(jnp.float32)
    src_grad[...] = jnp.zeros_like(src_grad)
    dst_grad[...] = jnp.zeros_like(dst_grad)
    live = count_ref[0, 0, round_index]
    row = lax.broadcasted_iota(jnp.int32, (TILE, TILE), 0)
    col = lax.broadcasted_iota(jnp.int32, (TILE, TILE), 1)
    shift = jnp.where(row == col, -0.5, 0.5).astype(jnp.float32)

    def step(group, carry):
        for lane in range(UNROLL):
            slot = group * UNROLL + lane
            code = code_ref[0, 0, round_index, slot]
            s = pl.multiple_of((code // 4) * TILE, TILE)
            e = pl.multiple_of((code % 4) * TILE, TILE)
            rel = rel_ref[pl.ds(rel_id_ref[0, 0, round_index, slot], 1), :]
            src_rel = (src_low[pl.ds(s, TILE), :] * rel).astype(jnp.bfloat16)
            dst = part_ref[pl.ds(e, TILE), :]
            scores = lax.dot_general(
                src_rel, dst, (((1,), (1,)), ((), ())), preferred_element_type=jnp.float32
            )
            on = jnp.where(slot < live, 1.0, 0.0).astype(jnp.float32)
            slope = ((jnp.tanh(scores * (0.5 * D**-0.5)) * 0.5 + shift) * on).astype(jnp.bfloat16)
            src_term = jnp.dot(slope, dst, preferred_element_type=jnp.float32)
            dst_term = lax.dot_general(
                slope, src_rel, (((0,), (0,)), ((), ())), preferred_element_type=jnp.float32
            )
            src_grad[pl.ds(s, TILE), :] += src_term * rel
            dst_grad[pl.ds(e, TILE), :] += dst_term
        return carry

    lax.fori_loop(0, (live + UNROLL - 1) // UNROLL, step, 0)
    diag = row == col
    for block in range(src_ref.shape[0] // TILE):
        at = slice(block * TILE, (block + 1) * TILE)
        table_out[at, :], state_out[block : block + 1, :] = adagrad_block(
            src_ref[at, :], state_ref[block : block + 1, :], src_grad[at, :] * D**-0.5, diag
        )
    dst_out[...] = (dst_grad[...] * D**-0.5).astype(jnp.bfloat16)


def tile_work(
    round_index, src_table, src_state, partition, tile_list, rel_list, live_count, rel_table
):
    smem = pl.BlockSpec(memory_space=pltpu.SMEM)
    vmem = pl.BlockSpec(memory_space=pltpu.VMEM)
    return pl.pallas_call(
        functools.partial(tile_kernel, round_index),
        out_shape=(
            jax.ShapeDtypeStruct(src_table.shape, jnp.float32),
            jax.ShapeDtypeStruct(src_state.shape, jnp.float32),
            jax.ShapeDtypeStruct(partition.shape, jnp.bfloat16),
        ),
        in_specs=[smem, smem, smem, vmem, vmem, vmem, vmem],
        out_specs=(vmem, vmem, vmem),
        scratch_shapes=[
            pltpu.VMEM(src_table.shape, jnp.float32),
            pltpu.VMEM(src_table.shape, jnp.float32),
            pltpu.VMEM(partition.shape, jnp.float32),
        ],
        compiler_params=pltpu.CompilerParams(vmem_limit_bytes=32 * 2**20),
    )(tile_list, rel_list, live_count, src_table, partition, rel_table, src_state)


def per_device(
    src_table, src_state, dst_table, dst_state, rel_table, partners, tiles, tile_rel, counts
):
    src_state = src_state.reshape(-1, TILE)
    dst_state = dst_state.reshape(-1, TILE)
    low = dst_table.astype(jnp.bfloat16)
    for round_index in range(ROUNDS):
        round_mask = partners[round_index, 0]
        first_id = round_index * 48
        moved = along_others(first_id, round_mask, low)
        partition = along_y(gathered, first_id + 16, round_mask, moved)
        src_table, src_state, dst_part = tile_work(
            round_index, src_table, src_state, partition, tiles, tile_rel, counts, rel_table
        )
        summed = along_y(reduced, first_id + 24, round_mask, dst_part)
        grad = along_others(first_id + 32, round_mask, summed)
        dst_table, dst_state, low = updated(dst_table, dst_state, grad)
    return (src_table, src_state.reshape(-1), dst_table, dst_state.reshape(-1))


def solution(mesh):
    in_specs = (
        P(("bucket", "rep"), None),
        P(("bucket", "rep")),
        P(("bucket", "rep"), None),
        P(("bucket", "rep")),
        P(),
        P(),
        P("bucket", "rep", None, None),
        P("bucket", "rep", None, None),
        P("bucket", "rep", None),
    )
    out_specs = (
        P(("bucket", "rep"), None),
        P(("bucket", "rep")),
        P(("bucket", "rep"), None),
        P(("bucket", "rep")),
    )
    return jax.shard_map(
        per_device, mesh=mesh, in_specs=in_specs, out_specs=out_specs, check_vma=False
    )
```

profile of v0, /device:TPU:1, one launch (start us, length us, event | category | flops | bytes accessed | tf_op | source)
XLA Modules:
  0.0 162.5 jit_solution(8056801007257132298)
XLA Ops:
  0.6 0.7 copy-done.8
  1.3 0.5 fusion
  5.7 0.9 convert_element_type.51
  6.6 6.6 %conditional.8 = (bf16[128,256]{1,0:T(8,128)(2,1)S(1)}) conditional(s32[]{:T(128)} %bitcast.1, bf16[128,256]{1,0:T(8,128)(2,1)S(1)} %convert_element_type.51, bf16[128,256]{1,0:T(8,128)(2,1)S(1)} %convert_element_type.51, bf16[128,256]{1,0:T(8,128)(2,1)S(1)} %convert_element_type.51, ...), branch_computations={%region_0.0_spmd, %region_1.0_spmd, %region_2.0_spmd, %region_3.0_... | conditional | bytes 131080 | solution.py:256
  6.7 6.6 %branch_13_fun.4 = bf16[128,256]{1,0:T(8,128)(2,1)S(1)} custom-call(bf16[128,256]{1,0:T(8,128)(2,1)S(1)} %copy.181.rows_ref), custom_call_target="tpu_custom_call" | custom-call | tf_op jit(solution)/shard_map/cond/branch_13_fun/pallas_call | solution.py:209
  13.3 0.0 copy-start.1
  13.3 0.0 copy-start.5
  13.3 23.3 %conditional.9 = (bf16[512,256]{1,0:T(8,128)(2,1)S(1)}) conditional(s32[]{:T(128)} %bitcast, bf16[128,256]{1,0:T(8,128)(2,1)S(1)} %get-tuple-element.228, bf16[128,256]{1,0:T(8,128)(2,1)S(1)} %get-tuple-element.228, bf16[128,256]{1,0:T(8,128)(2,1)S(1)} %get-tuple-element.228, ...), branch_computations={%region_16.0_spmd, %region_17.0_spmd, %region_18.0_spmd, %region_1... | conditional | bytes 8 | solution.py:249
  13.4 23.2 %branch_4_fun.9 = bf16[512,256]{1,0:T(8,128)(2,1)S(1)} custom-call(bf16[128,256]{1,0:T(8,128)(2,1)S(1)} %low_ref.4), custom_call_target="tpu_custom_call" | custom-call | tf_op jit(solution)/shard_map/cond/branch_4_fun/pallas_call | solution.py:93
  36.7 0.6 copy-done.3
  37.3 7.5 %shard_map.120 = (f32[512,256]{1,0:T(8,128)S(1)}, f32[4,128]{1,0:T(4,128)S(1)}, bf16[512,256]{1,0:T(8,128)(2,1)S(1)}) custom-call(s32[1,1,2,64]{3,2,1,0:T(2,128)S(1)} %copy-done.3, s32[1,1,2,64]{3,2,1,0:T(2,128)S(1)} %copy-done.4, s32[1,1,2]{2,1,0:T(1,128)S(1)} %copy-done.6, f32[512,256]{1,0:T(8,128)S(1)} %copy-done.1, ...), custom_call_target="tpu_custom_call" | custom-call | tf_op jit(solution)/shard_map/pallas_call | solution.py:310
  44.7 20.9 %conditional.10 = (bf16[128,256]{1,0:T(8,128)(2,1)S(1)}) conditional(s32[]{:T(128)} %bitcast, bf16[512,256]{1,0:T(8,128)(2,1)S(1)} %get-tuple-element.216, bf16[512,256]{1,0:T(8,128)(2,1)S(1)} %get-tuple-element.216, bf16[512,256]{1,0:T(8,128)(2,1)S(1)} %get-tuple-element.216, ...), branch_computations={%region_24.0_spmd, %region_25.0_spmd, %region_26.0_spmd, %region_2... | conditional | bytes 8 | solution.py:249
  44.8 20.9 %branch_4_fun.10 = bf16[128,256]{1,0:T(8,128)(2,1)S(1)} custom-call(bf16[512,256]{1,0:T(8,128)(2,1)S(1)} %part_ref.4), custom_call_target="tpu_custom_call" | custom-call | tf_op jit(solution)/shard_map/cond/branch_4_fun/pallas_call | solution.py:176
  65.7 0.0 copy-start
  65.7 21.0 %conditional.11 = (bf16[128,256]{1,0:T(8,128)(2,1)S(1)}) conditional(s32[]{:T(128)} %bitcast.1, bf16[128,256]{1,0:T(8,128)(2,1)S(1)} %get-tuple-element.230, bf16[128,256]{1,0:T(8,128)(2,1)S(1)} %get-tuple-element.230, bf16[128,256]{1,0:T(8,128)(2,1)S(1)} %get-tuple-element.230, ...), branch_computations={%region_32.0_spmd, %region_33.0_spmd, %region_34.0_spmd, %region_3... | conditional | bytes 131080 | solution.py:256
  65.7 20.9 %branch_13_fun.5 = bf16[128,256]{1,0:T(8,128)(2,1)S(1)} custom-call(bf16[128,256]{1,0:T(8,128)(2,1)S(1)} %copy.196.rows_ref), custom_call_target="tpu_custom_call" | custom-call | tf_op jit(solution)/shard_map/cond/branch_13_fun/pallas_call | solution.py:209
  86.7 0.6 copy-done.7
  87.3 0.1 shard_map.121
  87.5 31.4 %conditional.13 = (bf16[512,256]{1,0:T(8,128)(2,1)S(1)}) conditional(s32[]{:T(128)} %bitcast.3, bf16[128,256]{1,0:T(8,128)(2,1)S(1)} %get-tuple-element.232, bf16[128,256]{1,0:T(8,128)(2,1)S(1)} %get-tuple-element.232, bf16[128,256]{1,0:T(8,128)(2,1)S(1)} %get-tuple-element.232, ...), branch_computations={%region_64.0_spmd, %region_65.0_spmd, %region_66.0_spmd, %region_6... | conditional | bytes 8 | solution.py:249
  87.5 31.3 %branch_1_fun.13 = bf16[512,256]{1,0:T(8,128)(2,1)S(1)} custom-call(bf16[128,256]{1,0:T(8,128)(2,1)S(1)} %low_ref.9), custom_call_target="tpu_custom_call" | custom-call | tf_op jit(solution)/shard_map/cond/branch_1_fun/pallas_call | solution.py:93
  118.9 8.3 %shard_map.122 = (f32[512,256]{1,0:T(8,128)}, f32[4,128]{1,0:T(4,128)}, bf16[512,256]{1,0:T(8,128)(2,1)S(1)}) custom-call(s32[1,1,2,64]{3,2,1,0:T(2,128)S(1)} %copy-done.3, s32[1,1,2,64]{3,2,1,0:T(2,128)S(1)} %copy-done.4, s32[1,1,2]{2,1,0:T(1,128)S(1)} %copy-done.6, f32[512,256]{1,0:T(8,128)S(1)} %get-tuple-element.215.src_ref, ...), custom_call_target="tpu_custom_call" | custom-call | tf_op jit(solution)/shard_map/pallas_call | solution.py:310
  127.2 34.5 %conditional.14 = (bf16[128,256]{1,0:T(8,128)(2,1)S(1)}) conditional(s32[]{:T(128)} %bitcast.3, bf16[512,256]{1,0:T(8,128)(2,1)S(1)} %get-tuple-element.223, bf16[512,256]{1,0:T(8,128)(2,1)S(1)} %get-tuple-element.223, bf16[512,256]{1,0:T(8,128)(2,1)S(1)} %get-tuple-element.223, ...), branch_computations={%region_72.0_spmd, %region_73.0_spmd, %region_74.0_spmd, %region_7... | conditional | bytes 8 | solution.py:249
  127.2 34.4 %branch_1_fun.14 = bf16[128,256]{1,0:T(8,128)(2,1)S(1)} custom-call(bf16[512,256]{1,0:T(8,128)(2,1)S(1)} %part_ref.9), custom_call_target="tpu_custom_call" | custom-call | tf_op jit(solution)/shard_map/cond/branch_1_fun/pallas_call | solution.py:176
  161.7 0.8 shard_map.123
  (16 shorter events, 0.1 us)
Async XLA Ops:
  0.6 0.7 copy-start.8
  13.3 23.3 %copy-start.1 = (f32[512,256]{1,0:T(8,128)S(1)}, f32[512,256]{1,0:T(8,128)}, u32[]{:S(2)}) copy-start(f32[512,256]{1,0:T(8,128)} %src_ref.1) | copy-start | bytes 1572868
  13.3 23.3 %copy-start.2 = (f32[64,256]{1,0:T(8,128)S(1)}, f32[64,256]{1,0:T(8,128)}, u32[]{:S(2)}) copy-start(f32[64,256]{1,0:T(8,128)} %rel_ref.3) | copy-start | bytes 196612
  13.3 23.3 %copy-start.4 = (s32[1,1,2,64]{3,2,1,0:T(2,128)S(1)}, s32[1,1,2,64]{3,2,1,0:T(2,128)}, u32[]{:S(2)}) copy-start(s32[1,1,2,64]{3,2,1,0:T(2,128)} %rel_id_ref.3) | copy-start | bytes 1540
  13.3 23.3 %copy-start.5 = (f32[512]{0:T(512)S(1)}, f32[512]{0:T(512)}, u32[]{:S(2)}) copy-start(f32[512]{0:T(512)} %param.106) | copy-start | bytes 6148
  36.6 0.7 copy-start.3
  36.6 0.7 copy-start.6
  65.7 21.0 %copy-start = (f32[128,256]{1,0:T(8,128)S(1)}, f32[128,256]{1,0:T(8,128)}, u32[]{:S(2)}) copy-start(f32[128,256]{1,0:T(8,128)} %table_ref.1) | copy-start | bytes 393220
  86.6 0.7 copy-start.7
where the time goes:
time: 165 us; the launch traced here: 163 us
  Pallas kernels  154 us (93%)
  between operations  4.72 us (3%)
  local copies, waits for them, and re-layouts  2.5 us (2%)
    pallas_call x2, Pallas kernels, reduced(): pl.pallas_call(functools.partial(reduce_kernel, mask), out_shape=jax.Shap...  55.3 us
    pallas_call x2, Pallas kernels, gathered(): pl.pallas_call(functools.partial(gather_kernel, mask), out_shape=jax.Shap...  54.6 us
    pallas_call x2, Pallas kernels, permuted(): pl.pallas_call(functools.partial(permute_kernel, mask), out_shape=jax.Sha...  27.4 us
    pallas_call x2, Pallas kernels, tile_work(): pl.pallas_call(functools.partial(tile_kernel, round_index), out_shape=(ja...  15.7 us

commit v1 on v0

--- a/solution.py
+++ b/solution.py
@@ -249,9 +249,9 @@
     return lax.switch((round_mask >> 2) & 7, branches, block)
 
 
-def along_others(first_id, round_mask, block):
+def along_others(round_mask, block):
     branches = [
-        functools.partial(permuted, mask, first_id + i) for i, mask in enumerate(OTHER_MASKS)
+        functools.partial(permuted, mask, i) for i, mask in enumerate(OTHER_MASKS)
     ]
     return lax.switch((round_mask >> 5) * 4 + (round_mask & 3), branches, block)
 
@@ -333,14 +333,13 @@
     low = dst_table.astype(jnp.bfloat16)
     for round_index in range(ROUNDS):
         round_mask = partners[round_index, 0]
-        first_id = round_index * 48
-        moved = along_others(first_id, round_mask, low)
-        partition = along_y(gathered, first_id + 16, round_mask, moved)
+        moved = along_others(round_mask, low)
+        partition = along_y(gathered, 16, round_mask, moved)
         src_table, src_state, dst_part = tile_work(
             round_index, src_table, src_state, partition, tiles, tile_rel, counts, rel_table
         )
-        summed = along_y(reduced, first_id + 24, round_mask, dst_part)
-        grad = along_others(first_id + 32, round_mask, summed)
+        summed = along_y(reduced, 24, round_mask, dst_part)
+        grad = along_others(round_mask, summed)
         dst_table, dst_state, low = updated(dst_table, dst_state, grad)
     return (src_table, src_state.reshape(-1), dst_table, dst_state.reshape(-1))
 

time: 165 us -> 124 us (0.75)
  the two profiles are of different devices: /device:TPU:1 before, /device:TPU:72 now
where the time goes in v1:
time: 124 us
  Pallas kernels  115 us (93%)
  between operations  4.72 us (4%)
  local copies, waits for them, and re-layouts  2.52 us (2%)
    pallas_call x2, Pallas kernels, reduced(): pl.pallas_call(functools.partial(reduce_kernel, mask), out_shape=jax.Shap...  45.5 us
    pallas_call x2, Pallas kernels, gathered(): pl.pallas_call(functools.partial(gather_kernel, mask), out_shape=jax.Shap...  35.2 us
    pallas_call x4, Pallas kernels, permuted(): pl.pallas_call(functools.partial(permute_kernel, mask), out_shape=jax.Sha...  21.9 us
    pallas_call x2, Pallas kernels, tile_work(): pl.pallas_call(functools.partial(tile_kernel, round_index), out_shape=(ja...  11.6 us

profile of v1, /device:TPU:72, one launch (start us, length us, event | category | flops | bytes accessed | tf_op | source)
XLA Modules:
  0.0 123.7 jit_solution(12071674852560676583)
XLA Ops:
  0.6 0.7 copy-done.8
  1.3 0.5 fusion
  5.7 0.9 convert_element_type.51
  6.6 5.1 %conditional.8 = (bf16[128,256]{1,0:T(8,128)(2,1)S(1)}) conditional(s32[]{:T(128)} %bitcast.1, bf16[128,256]{1,0:T(8,128)(2,1)S(1)} %convert_element_type.51, bf16[128,256]{1,0:T(8,128)(2,1)S(1)} %convert_element_type.51, bf16[128,256]{1,0:T(8,128)(2,1)S(1)} %convert_element_type.51, ...), branch_computations={%region_0.0_spmd, %region_1.0_spmd, %region_2.0_spmd, %region_3.0_... | conditional | bytes 131080 | solution.py:256
  6.7 5.0 %branch_2_fun.8 = bf16[128,256]{1,0:T(8,128)(2,1)S(1)} custom-call(bf16[128,256]{1,0:T(8,128)(2,1)S(1)} %copy.170.rows_ref), custom_call_target="tpu_custom_call" | custom-call | tf_op jit(solution)/shard_map/cond/branch_2_fun/pallas_call | solution.py:209
  11.8 24.5 %conditional.9 = (bf16[512,256]{1,0:T(8,128)(2,1)S(1)}) conditional(s32[]{:T(128)} %bitcast, bf16[128,256]{1,0:T(8,128)(2,1)S(1)} %get-tuple-element.228, bf16[128,256]{1,0:T(8,128)(2,1)S(1)} %get-tuple-element.228, bf16[128,256]{1,0:T(8,128)(2,1)S(1)} %get-tuple-element.228, ...), branch_computations={%region_16.0_spmd, %region_17.0_spmd, %region_18.0_spmd, %region_1... | conditional | bytes 8 | solution.py:249
  11.8 24.4 %branch_4_fun.9 = bf16[512,256]{1,0:T(8,128)(2,1)S(1)} custom-call(bf16[128,256]{1,0:T(8,128)(2,1)S(1)} %low_ref.4), custom_call_target="tpu_custom_call" | custom-call | tf_op jit(solution)/shard_map/cond/branch_4_fun/pallas_call | solution.py:93
  36.3 0.6 copy-done.3
  36.9 7.4 %shard_map.120 = (f32[512,256]{1,0:T(8,128)S(1)}, f32[4,128]{1,0:T(4,128)S(1)}, bf16[512,256]{1,0:T(8,128)(2,1)S(1)}) custom-call(s32[1,1,2,64]{3,2,1,0:T(2,128)S(1)} %copy-done.3, s32[1,1,2,64]{3,2,1,0:T(2,128)S(1)} %copy-done.4, s32[1,1,2]{2,1,0:T(1,128)S(1)} %copy-done.6, f32[512,256]{1,0:T(8,128)S(1)} %copy-done.1, ...), custom_call_target="tpu_custom_call" | custom-call | tf_op jit(solution)/shard_map/pallas_call | solution.py:310
  44.4 23.3 %conditional.10 = (bf16[128,256]{1,0:T(8,128)(2,1)S(1)}) conditional(s32[]{:T(128)} %bitcast, bf16[512,256]{1,0:T(8,128)(2,1)S(1)} %get-tuple-element.216, bf16[512,256]{1,0:T(8,128)(2,1)S(1)} %get-tuple-element.216, bf16[512,256]{1,0:T(8,128)(2,1)S(1)} %get-tuple-element.216, ...), branch_computations={%region_24.0_spmd, %region_25.0_spmd, %region_26.0_spmd, %region_2... | conditional | bytes 8 | solution.py:249
  44.4 23.2 %branch_4_fun.10 = bf16[128,256]{1,0:T(8,128)(2,1)S(1)} custom-call(bf16[512,256]{1,0:T(8,128)(2,1)S(1)} %part_ref.4), custom_call_target="tpu_custom_call" | custom-call | tf_op jit(solution)/shard_map/cond/branch_4_fun/pallas_call | solution.py:176
  67.7 5.1 %conditional.11 = (bf16[128,256]{1,0:T(8,128)(2,1)S(1)}) conditional(s32[]{:T(128)} %bitcast.1, bf16[128,256]{1,0:T(8,128)(2,1)S(1)} %get-tuple-element.230, bf16[128,256]{1,0:T(8,128)(2,1)S(1)} %get-tuple-element.230, bf16[128,256]{1,0:T(8,128)(2,1)S(1)} %get-tuple-element.230, ...), branch_computations={%region_32.0_spmd, %region_33.0_spmd, %region_34.0_spmd, %region_3... | conditional | bytes 131080 | solution.py:256
  67.7 5.0 %branch_2_fun.11 = bf16[128,256]{1,0:T(8,128)(2,1)S(1)} custom-call(bf16[128,256]{1,0:T(8,128)(2,1)S(1)} %copy.185.rows_ref), custom_call_target="tpu_custom_call" | custom-call | tf_op jit(solution)/shard_map/cond/branch_2_fun/pallas_call | solution.py:209
  72.8 0.6 copy-done.7
  73.5 6.3 %conditional.12 = (bf16[128,256]{1,0:T(8,128)(2,1)S(1)}) conditional(s32[]{:T(128)} %bitcast.4, bf16[128,256]{1,0:T(8,128)(2,1)S(1)} %get-tuple-element.217, bf16[128,256]{1,0:T(8,128)(2,1)S(1)} %get-tuple-element.217, bf16[128,256]{1,0:T(8,128)(2,1)S(1)} %get-tuple-element.217, ...), branch_computations={%region_48.0_spmd, %region_49.0_spmd, %region_50.0_spmd, %region_5... | conditional | bytes 131080 | solution.py:256
  73.6 6.2 %branch_13_fun.6 = bf16[128,256]{1,0:T(8,128)(2,1)S(1)} custom-call(bf16[128,256]{1,0:T(8,128)(2,1)S(1)} %copy.211.rows_ref), custom_call_target="tpu_custom_call" | custom-call | tf_op jit(solution)/shard_map/cond/branch_13_fun/pallas_call | solution.py:209
  79.9 10.8 %conditional.13 = (bf16[512,256]{1,0:T(8,128)(2,1)S(1)}) conditional(s32[]{:T(128)} %bitcast.3, bf16[128,256]{1,0:T(8,128)(2,1)S(1)} %get-tuple-element.232, bf16[128,256]{1,0:T(8,128)(2,1)S(1)} %get-tuple-element.232, bf16[128,256]{1,0:T(8,128)(2,1)S(1)} %get-tuple-element.232, ...), branch_computations={%region_64.0_spmd, %region_65.0_spmd, %region_66.0_spmd, %region_6... | conditional | bytes 8 | solution.py:249
  79.9 10.8 %branch_0_fun.6 = bf16[512,256]{1,0:T(8,128)(2,1)S(1)} custom-call(bf16[128,256]{1,0:T(8,128)(2,1)S(1)} %low_ref.8), custom_call_target="tpu_custom_call" | custom-call | tf_op jit(solution)/shard_map/cond/branch_0_fun/pallas_call | solution.py:93
  90.7 4.2 %shard_map.122 = (f32[512,256]{1,0:T(8,128)}, f32[4,128]{1,0:T(4,128)}, bf16[512,256]{1,0:T(8,128)(2,1)S(1)}) custom-call(s32[1,1,2,64]{3,2,1,0:T(2,128)S(1)} %copy-done.3, s32[1,1,2,64]{3,2,1,0:T(2,128)S(1)} %copy-done.4, s32[1,1,2]{2,1,0:T(1,128)S(1)} %copy-done.6, f32[512,256]{1,0:T(8,128)S(1)} %get-tuple-element.215.src_ref, ...), custom_call_target="tpu_custom_call" | custom-call | tf_op jit(solution)/shard_map/pallas_call | solution.py:310
  94.9 22.3 %conditional.14 = (bf16[128,256]{1,0:T(8,128)(2,1)S(1)}) conditional(s32[]{:T(128)} %bitcast.3, bf16[512,256]{1,0:T(8,128)(2,1)S(1)} %get-tuple-element.223, bf16[512,256]{1,0:T(8,128)(2,1)S(1)} %get-tuple-element.223, bf16[512,256]{1,0:T(8,128)(2,1)S(1)} %get-tuple-element.223, ...), branch_computations={%region_72.0_spmd, %region_73.0_spmd, %region_74.0_spmd, %region_7... | conditional | bytes 8 | solution.py:249
  94.9 22.3 %branch_0_fun.7 = bf16[128,256]{1,0:T(8,128)(2,1)S(1)} custom-call(bf16[512,256]{1,0:T(8,128)(2,1)S(1)} %part_ref.8), custom_call_target="tpu_custom_call" | custom-call | tf_op jit(solution)/shard_map/cond/branch_0_fun/pallas_call | solution.py:176
  117.2 5.7 %conditional.15 = (bf16[128,256]{1,0:T(8,128)(2,1)S(1)}) conditional(s32[]{:T(128)} %bitcast.4, bf16[128,256]{1,0:T(8,128)(2,1)S(1)} %get-tuple-element.234, bf16[128,256]{1,0:T(8,128)(2,1)S(1)} %get-tuple-element.234, bf16[128,256]{1,0:T(8,128)(2,1)S(1)} %get-tuple-element.234, ...), branch_computations={%region_80.0_spmd, %region_81.0_spmd, %region_82.0_spmd, %region_8... | conditional | bytes 131080 | solution.py:256
  117.2 5.6 %branch_13_fun.7 = bf16[128,256]{1,0:T(8,128)(2,1)S(1)} custom-call(bf16[128,256]{1,0:T(8,128)(2,1)S(1)} %copy.226.rows_ref), custom_call_target="tpu_custom_call" | custom-call | tf_op jit(solution)/shard_map/cond/branch_13_fun/pallas_call | solution.py:209
  122.9 0.8 shard_map.123
  (20 shorter events, 0.2 us)
Async XLA Ops:
  0.6 0.7 copy-start.8
  11.7 24.5 %copy-start.1 = (f32[512,256]{1,0:T(8,128)S(1)}, f32[512,256]{1,0:T(8,128)}, u32[]{:S(2)}) copy-start(f32[512,256]{1,0:T(8,128)} %src_ref.1) | copy-start | bytes 1572868
  11.7 24.5 %copy-start.2 = (f32[64,256]{1,0:T(8,128)S(1)}, f32[64,256]{1,0:T(8,128)}, u32[]{:S(2)}) copy-start(f32[64,256]{1,0:T(8,128)} %rel_ref.3) | copy-start | bytes 196612
  11.7 24.5 %copy-start.4 = (s32[1,1,2,64]{3,2,1,0:T(2,128)S(1)}, s32[1,1,2,64]{3,2,1,0:T(2,128)}, u32[]{:S(2)}) copy-start(s32[1,1,2,64]{3,2,1,0:T(2,128)} %rel_id_ref.3) | copy-start | bytes 1540
  11.8 24.5 %copy-start.5 = (f32[512]{0:T(512)S(1)}, f32[512]{0:T(512)}, u32[]{:S(2)}) copy-start(f32[512]{0:T(512)} %param.106) | copy-start | bytes 6148
  36.2 0.7 copy-start.3
  36.2 0.7 copy-start.6
  67.6 5.1 %copy-start = (f32[128,256]{1,0:T(8,128)S(1)}, f32[128,256]{1,0:T(8,128)}, u32[]{:S(2)}) copy-start(f32[128,256]{1,0:T(8,128)} %table_ref.1) | copy-start | bytes 393220
  72.7 0.7 copy-start.7

commit v2 on v1

--- a/solution.py
+++ b/solution.py
@@ -15,7 +15,8 @@
 learn_rate = 0.1
 
 
-HALF = TILE // 2
+CHUNK = TILE // 4
+ORDER = (0, 2, 1, 3)
 MESH = pl.DeviceIdType.MESH
 
 
@@ -40,8 +41,8 @@
     pl.semaphore_wait(barrier, len(devices))
 
 
-def rows(quarter, half):
-    return pl.ds(pl.multiple_of(quarter * TILE + half * HALF, HALF), HALF)
+def rows(quarter, chunk):
+    return pl.ds(pl.multiple_of(quarter * TILE + chunk * CHUNK, CHUNK), CHUNK)
 
 
 def gather_kernel(mask, low_ref, part_ref, send, recv):
@@ -54,37 +55,36 @@
         )
 
     greet((to_pair, to_left, to_right) if mask else (to_left, to_right))
-    own = [part_ref.at[rows(me, half)] for half in range(2)]
+    own = [part_ref.at[rows(me, chunk)] for chunk in range(4)]
+    hop = {}
     if mask:
-        hop = [copy(half, low_ref.at[rows(0, half)], own[half], to_pair) for half in range(2)]
-        hop[0].start()
-        hop[1].start()
+        for chunk in ORDER:
+            hop[chunk] = copy(chunk, low_ref.at[rows(0, chunk)], own[chunk], to_pair)
+            hop[chunk].start()
     else:
         part_ref[pl.ds(pl.multiple_of(me * TILE, TILE), TILE), :] = low_ref[...]
-        hop = []
-    going_right = [copy(2 + half, own[half], own[half], to_right) for half in range(2)]
-    going_left = [copy(4 + half, own[half], own[half], to_left) for half in range(2)]
-    if mask:
-        hop[0].wait_recv()
-    going_right[0].start()
-    going_left[0].start()
-    if mask:
-        hop[1].wait_recv()
-    going_left[1].start()
-    going_right[1].start()
-    passed = part_ref.at[rows(left, 0)]
-    on_right = copy(6, passed, passed, to_right)
-    going_right[0].wait_recv()
-    on_right.start()
-    passed = part_ref.at[rows(right, 1)]
-    on_left = copy(7, passed, passed, to_left)
-    going_left[1].wait_recv()
-    on_left.start()
-    going_left[0].wait_recv()
-    going_right[1].wait_recv()
-    on_right.wait_recv()
-    on_left.wait_recv()
-    for sent in (*hop, *going_right, *going_left, on_right, on_left):
+    going_right = [copy(4 + chunk, own[chunk], own[chunk], to_right) for chunk in range(4)]
+    going_left = [copy(8 + chunk, own[chunk], own[chunk], to_left) for chunk in range(4)]
+    for chunk in ORDER:
+        if mask:
+            hop[chunk].wait_recv()
+        near = (going_right, going_left) if chunk < 2 else (going_left, going_right)
+        near[0][chunk].start()
+        near[1][chunk].start()
+    onward = []
+    for chunk in ORDER:
+        came, source, device = (
+            (going_right, left, to_right) if chunk < 2 else (going_left, right, to_left)
+        )
+        came[chunk].wait_recv()
+        passed = part_ref.at[rows(source, chunk)]
+        onward.append(copy(12 + chunk, passed, passed, device))
+        onward[-1].start()
+    for chunk in range(4):
+        (going_left if chunk < 2 else going_right)[chunk].wait_recv()
+    for passed in onward:
+        passed.wait_recv()
+    for sent in (*hop.values(), *going_right, *going_left, *onward):
         sent.wait_send()
 
 
@@ -95,7 +95,7 @@
         out_shape=jax.ShapeDtypeStruct((4 * TILE, D), jnp.bfloat16),
         in_specs=[vmem],
         out_specs=vmem,
-        scratch_shapes=[pltpu.SemaphoreType.DMA((8,)), pltpu.SemaphoreType.DMA((8,))],
+        scratch_shapes=[pltpu.SemaphoreType.DMA((16,)), pltpu.SemaphoreType.DMA((16,))],
         compiler_params=pltpu.CompilerParams(
             collective_id=collective_id, has_side_effects=True, vmem_limit_bytes=16 * 2**20
         ),
@@ -130,44 +130,43 @@
         return ref[...].astype(jnp.float32)
 
     greet((to_pair, to_left, to_right) if mask else (to_left, to_right))
-    first = copy(0, part_ref.at[rows(far, 0)], relay.at[rows(0, 0)], to_left)
-    second = copy(1, part_ref.at[rows(far, 1)], relay.at[rows(0, 1)], to_right)
-    left_one = copy(2, part_ref.at[rows(left, 1)], side.at[rows(1, 1)], to_left)
-    right_zero = copy(3, part_ref.at[rows(right, 0)], side.at[rows(0, 0)], to_right)
-    left_zero = copy(4, added.at[rows(0, 0)], side.at[rows(1, 0)], to_left)
-    right_one = copy(5, added.at[rows(0, 1)], side.at[rows(0, 1)], to_right)
-    if mask:
-        back = [copy(6 + half, total.at[rows(0, half)], got.at[rows(0, half)], to_pair) for half in range(2)]
-    else:
-        back, total = [], got
-    first.start()
-    second.start()
-    left_one.start()
-    right_zero.start()
-    first.wait_recv()
-    added[rows(0, 0), :] = (
-        wide(relay.at[rows(0, 0)]) + wide(part_ref.at[rows(left, 0)])
-    ).astype(jnp.bfloat16)
-    left_zero.start()
-    second.wait_recv()
-    added[rows(0, 1), :] = (
-        wide(relay.at[rows(0, 1)]) + wide(part_ref.at[rows(right, 1)])
-    ).astype(jnp.bfloat16)
-    right_one.start()
-    for half, needed in ((0, (right_zero, left_zero)), (1, (left_one, right_one))):
-        needed[0].wait_recv()
-        needed[1].wait_recv()
-        total[rows(0, half), :] = (
-            wide(part_ref.at[rows(me, half)])
-            + wide(side.at[rows(0, half)])
-            + wide(side.at[rows(1, half)])
+    far_ones, near_ones, added_ones, back = {}, {}, {}, {}
+    for chunk in ORDER:
+        device = to_left if chunk < 2 else to_right
+        far_ones[chunk] = copy(chunk, part_ref.at[rows(far, chunk)], relay.at[rows(0, chunk)], device)
+        far_ones[chunk].start()
+    for chunk in ORDER:
+        owner, place, device = (right, 0, to_right) if chunk < 2 else (left, 1, to_left)
+        near_ones[chunk] = copy(
+            4 + chunk, part_ref.at[rows(owner, chunk)], side.at[rows(place, chunk)], device
+        )
+        near_ones[chunk].start()
+    for chunk in ORDER:
+        owner, place, device = (left, 1, to_left) if chunk < 2 else (right, 0, to_right)
+        far_ones[chunk].wait_recv()
+        added[rows(0, chunk), :] = (
+            wide(relay.at[rows(0, chunk)]) + wide(part_ref.at[rows(owner, chunk)])
+        ).astype(jnp.bfloat16)
+        added_ones[chunk] = copy(
+            8 + chunk, added.at[rows(0, chunk)], side.at[rows(place, chunk)], device
+        )
+        added_ones[chunk].start()
+    for chunk in ORDER:
+        near_ones[chunk].wait_recv()
+        added_ones[chunk].wait_recv()
+        (total if mask else got)[rows(0, chunk), :] = (
+            wide(part_ref.at[rows(me, chunk)])
+            + wide(side.at[rows(0, chunk)])
+            + wide(side.at[rows(1, chunk)])
         ).astype(jnp.bfloat16)
         if mask:
-            back[half].start()
-    for sent in back:
+            back[chunk] = copy(12 + chunk, total.at[rows(0, chunk)], got.at[rows(0, chunk)], to_pair)
+            back[chunk].start()
+    for sent in back.values():
         sent.wait_recv()
-    for sent in (first, second, left_one, right_zero, left_zero, right_one, *back):
-        sent.wait_send()
+    for group in (far_ones, near_ones, added_ones, back):
+        for sent in group.values():
+            sent.wait_send()
 
 
 def reduced(mask, collective_id, dst_part):
@@ -183,8 +182,8 @@
             pltpu.VMEM((TILE, D), low),
             pltpu.VMEM((2 * TILE, D), low),
             pltpu.VMEM((TILE, D), low),
-            pltpu.SemaphoreType.DMA((8,)),
-            pltpu.SemaphoreType.DMA((8,)),
+            pltpu.SemaphoreType.DMA((16,)),
+            pltpu.SemaphoreType.DMA((16,)),
         ],
         compiler_params=pltpu.CompilerParams(
             collective_id=collective_id, has_side_effects=True, vmem_limit_bytes=16 * 2**20
@@ -244,19 +243,41 @@
 OTHER_MASKS = tuple((x << 5) + low for x in range(4) for low in range(4))
 
 
-def along_y(make, first_id, round_mask, block):
+def along_y(make, first_id, index, block):
     branches = [functools.partial(make, mask, first_id + i) for i, mask in enumerate(Y_MASKS)]
-    return lax.switch((round_mask >> 2) & 7, branches, block)
-
-
-def along_others(round_mask, block):
-    branches = [
-        functools.partial(permuted, mask, i) for i, mask in enumerate(OTHER_MASKS)
-    ]
-    return lax.switch((round_mask >> 5) * 4 + (round_mask & 3), branches, block)
-
-
-UNROLL = 4
+    return lax.switch(index, branches, block)
+
+
+def along_others(index, block):
+    branches = [functools.partial(permuted, mask, i) for i, mask in enumerate(OTHER_MASKS)]
+    return lax.switch(index, branches, block)
+
+
+def prepare_kernel(partners_ref, table_ref, low_ref, *index_refs):
+    low_ref[...] = table_ref[...].astype(jnp.bfloat16)
+    for round_index in range(ROUNDS):
+        mask = partners_ref[round_index, 0]
+        index_refs[2 * round_index][0, 0] = (mask >> 5) * 4 + (mask & 3)
+        index_refs[2 * round_index + 1][0, 0] = (mask >> 2) & 7
+
+
+def prepared(partners, table):
+    smem = pl.BlockSpec(memory_space=pltpu.SMEM)
+    vmem = pl.BlockSpec(memory_space=pltpu.VMEM)
+    low, *indices = pl.pallas_call(
+        prepare_kernel,
+        out_shape=(
+            jax.ShapeDtypeStruct(table.shape, jnp.bfloat16),
+            *[jax.ShapeDtypeStruct((1, 1), jnp.int32)] * (2 * ROUNDS),
+        ),
+        in_specs=[smem, vmem],
+        out_specs=(vmem, *[smem] * (2 * ROUNDS)),
+        compiler_params=pltpu.CompilerParams(vmem_limit_bytes=16 * 2**20),
+    )(partners, table)
+    return low, [index[0, 0] for index in indices]
+
+
+UNROLL = 16
 
 
 def tile_kernel(round_index, code_ref, rel_id_ref, count_ref, src_ref, part_ref, rel_ref, state_ref,
@@ -271,25 +292,37 @@
     shift = jnp.where(row == col, -0.5, 0.5).astype(jnp.float32)
 
     def step(group, carry):
-        for lane in range(UNROLL):
-            slot = group * UNROLL + lane
-            code = code_ref[0, 0, round_index, slot]
-            s = pl.multiple_of((code // 4) * TILE, TILE)
-            e = pl.multiple_of((code % 4) * TILE, TILE)
-            rel = rel_ref[pl.ds(rel_id_ref[0, 0, round_index, slot], 1), :]
-            src_rel = (src_low[pl.ds(s, TILE), :] * rel).astype(jnp.bfloat16)
-            dst = part_ref[pl.ds(e, TILE), :]
-            scores = lax.dot_general(
-                src_rel, dst, (((1,), (1,)), ((), ())), preferred_element_type=jnp.float32
+        lanes = range(UNROLL)
+        slots = [group * UNROLL + lane for lane in lanes]
+        codes = [code_ref[0, 0, round_index, slot] for slot in slots]
+        src_at = [pl.ds(pl.multiple_of((code // 4) * TILE, TILE), TILE) for code in codes]
+        dst_at = [pl.ds(pl.multiple_of((code % 4) * TILE, TILE), TILE) for code in codes]
+        rels = [rel_ref[pl.ds(rel_id_ref[0, 0, round_index, slot], 1), :] for slot in slots]
+        dsts = [part_ref[at, :] for at in dst_at]
+        src_rels = [(src_low[src_at[lane], :] * rels[lane]).astype(jnp.bfloat16) for lane in lanes]
+        scores = [
+            lax.dot_general(
+                src_rels[lane], dsts[lane], (((1,), (1,)), ((), ())), preferred_element_type=jnp.float32
             )
-            on = jnp.where(slot < live, 1.0, 0.0).astype(jnp.float32)
-            slope = ((jnp.tanh(scores * (0.5 * D**-0.5)) * 0.5 + shift) * on).astype(jnp.bfloat16)
-            src_term = jnp.dot(slope, dst, preferred_element_type=jnp.float32)
-            dst_term = lax.dot_general(
-                slope, src_rel, (((0,), (0,)), ((), ())), preferred_element_type=jnp.float32
+            for lane in lanes
+        ]
+        ons = [jnp.where(slot < live, 1.0, 0.0).astype(jnp.float32) for slot in slots]
+        slopes = [
+            ((jnp.tanh(scores[lane] * (0.5 * D**-0.5)) * 0.5 + shift) * ons[lane]).astype(jnp.bfloat16)
+            for lane in lanes
+        ]
+        src_terms = [
+            jnp.dot(slopes[lane], dsts[lane], preferred_element_type=jnp.float32) for lane in lanes
+        ]
+        dst_terms = [
+            lax.dot_general(
+                slopes[lane], src_rels[lane], (((0,), (0,)), ((), ())), preferred_element_type=jnp.float32
             )
-            src_grad[pl.ds(s, TILE), :] += src_term * rel
-            dst_grad[pl.ds(e, TILE), :] += dst_term
+            for lane in lanes
+        ]
+        for lane in lanes:
+            src_grad[src_at[lane], :] += src_terms[lane] * rels[lane]
+            dst_grad[dst_at[lane], :] += dst_terms[lane]
         return carry
 
     lax.fori_loop(0, (live + UNROLL - 1) // UNROLL, step, 0)
@@ -330,16 +363,16 @@
 ):
     src_state = src_state.reshape(-1, TILE)
     dst_state = dst_state.reshape(-1, TILE)
-    low = dst_table.astype(jnp.bfloat16)
+    low, indices = prepared(partners, dst_table)
     for round_index in range(ROUNDS):
-        round_mask = partners[round_index, 0]
-        moved = along_others(round_mask, low)
-        partition = along_y(gathered, 16, round_mask, moved)
+        others, y = indices[2 * round_index : 2 * round_index + 2]
+        moved = along_others(others, low)
+        partition = along_y(gathered, 16, y, moved)
         src_table, src_state, dst_part = tile_work(
             round_index, src_table, src_state, partition, tiles, tile_rel, counts, rel_table
         )
-        summed = along_y(reduced, 24, round_mask, dst_part)
-        grad = along_others(round_mask, summed)
+        summed = along_y(reduced, 24, y, dst_part)
+        grad = along_others(others, summed)
         dst_table, dst_state, low = updated(dst_table, dst_state, grad)
     return (src_table, src_state.reshape(-1), dst_table, dst_state.reshape(-1))
 

time: 124 us -> 112 us (0.903)
  the two profiles are of different devices: /device:TPU:72 before, /device:TPU:17 now
where the time goes in v2:
time: 112 us
  Pallas kernels  105 us (94%)
  between operations  3.43 us (3%)
  local copies, waits for them, and re-layouts  2.9 us (3%)
    pallas_call x2, Pallas kernels, gathered(): pl.pallas_call(functools.partial(gather_kernel, mask), out_shape=jax.Shap...  34.1 us
    pallas_call x4, Pallas kernels, permuted(): pl.pallas_call(functools.partial(permute_kernel, mask), out_shape=jax.Sha...  32.9 us
    pallas_call x2, Pallas kernels, reduced(): pl.pallas_call(functools.partial(reduce_kernel, mask), out_shape=jax.Shap...  24.9 us
    pallas_call x2, Pallas kernels, tile_work(): pl.pallas_call(functools.partial(tile_kernel, round_index), out_shape=(ja...  11.2 us
    unnamed x20, local copies, waits for them, and re-layouts  2.88 us

profile of v2, /device:TPU:17, one launch (start us, length us, event | category | flops | bytes accessed | tf_op | source)
XLA Modules:
  0.0 112.0 jit_solution(11147194053159054856)
XLA Ops:
  0.6 0.7 copy-done.8
  1.3 0.9 copy-done.1
  2.2 1.1 shard_map.120
  5.9 3.9 %conditional.8 = (bf16[128,256]{1,0:T(8,128)(2,1)S(1)}) conditional(s32[]{:T(128)} %bitcast.1, bf16[128,256]{1,0:T(8,128)(2,1)S(1)} %get-tuple-element.222, bf16[128,256]{1,0:T(8,128)(2,1)S(1)} %get-tuple-element.222, bf16[128,256]{1,0:T(8,128)(2,1)S(1)} %get-tuple-element.222, ...), branch_computations={%region_0.0_spmd, %region_1.0_spmd, %region_2.0_spmd, %region_3.0_... | conditional | bytes 131080 | solution.py:253
  6.0 3.8 %branch_4_fun.8 = bf16[128,256]{1,0:T(8,128)(2,1)S(1)} custom-call(bf16[128,256]{1,0:T(8,128)(2,1)S(1)} %copy.172.rows_ref), custom_call_target="tpu_custom_call" | custom-call | tf_op jit(solution)/shard_map/cond/branch_4_fun/pallas_call | solution.py:208
  9.9 21.5 %conditional.9 = (bf16[512,256]{1,0:T(8,128)(2,1)S(1)}) conditional(s32[]{:T(128)} %bitcast, bf16[128,256]{1,0:T(8,128)(2,1)S(1)} %get-tuple-element.236, bf16[128,256]{1,0:T(8,128)(2,1)S(1)} %get-tuple-element.236, bf16[128,256]{1,0:T(8,128)(2,1)S(1)} %get-tuple-element.236, ...), branch_computations={%region_16.0_spmd, %region_17.0_spmd, %region_18.0_spmd, %region_1... | conditional | bytes 8 | solution.py:248
  9.9 21.5 %branch_6_fun.9 = bf16[512,256]{1,0:T(8,128)(2,1)S(1)} custom-call(bf16[128,256]{1,0:T(8,128)(2,1)S(1)} %low_ref.6), custom_call_target="tpu_custom_call" | custom-call | tf_op jit(solution)/shard_map/cond/branch_6_fun/pallas_call | solution.py:93
  31.5 0.6 copy-done.4
  32.1 5.2 %shard_map.121 = (f32[512,256]{1,0:T(8,128)S(1)}, f32[4,128]{1,0:T(4,128)S(1)}, bf16[512,256]{1,0:T(8,128)(2,1)S(1)}) custom-call(s32[1,1,2,64]{3,2,1,0:T(2,128)S(1)} %copy-done.4, s32[1,1,2,64]{3,2,1,0:T(2,128)S(1)} %copy-done.5, s32[1,1,2]{2,1,0:T(1,128)S(1)} %copy-done.7, f32[512,256]{1,0:T(8,128)S(1)} %copy-done, ...), custom_call_target="tpu_custom_call" | custom-call | tf_op jit(solution)/shard_map/pallas_call | solution.py:343
  37.3 12.4 %conditional.10 = (bf16[128,256]{1,0:T(8,128)(2,1)S(1)}) conditional(s32[]{:T(128)} %bitcast, bf16[512,256]{1,0:T(8,128)(2,1)S(1)} %get-tuple-element.226, bf16[512,256]{1,0:T(8,128)(2,1)S(1)} %get-tuple-element.226, bf16[512,256]{1,0:T(8,128)(2,1)S(1)} %get-tuple-element.226, ...), branch_computations={%region_24.0_spmd, %region_25.0_spmd, %region_26.0_spmd, %region_2... | conditional | bytes 8 | solution.py:248
  37.4 12.4 %branch_6_fun.10 = bf16[128,256]{1,0:T(8,128)(2,1)S(1)} custom-call(bf16[512,256]{1,0:T(8,128)(2,1)S(1)} %part_ref.6), custom_call_target="tpu_custom_call" | custom-call | tf_op jit(solution)/shard_map/cond/branch_6_fun/pallas_call | solution.py:175
  49.8 3.9 %conditional.11 = (bf16[128,256]{1,0:T(8,128)(2,1)S(1)}) conditional(s32[]{:T(128)} %bitcast.1, bf16[128,256]{1,0:T(8,128)(2,1)S(1)} %get-tuple-element.238, bf16[128,256]{1,0:T(8,128)(2,1)S(1)} %get-tuple-element.238, bf16[128,256]{1,0:T(8,128)(2,1)S(1)} %get-tuple-element.238, ...), branch_computations={%region_32.0_spmd, %region_33.0_spmd, %region_34.0_spmd, %region_3... | conditional | bytes 131080 | solution.py:253
  49.8 3.8 %branch_4_fun.11 = bf16[128,256]{1,0:T(8,128)(2,1)S(1)} custom-call(bf16[128,256]{1,0:T(8,128)(2,1)S(1)} %copy.187.rows_ref), custom_call_target="tpu_custom_call" | custom-call | tf_op jit(solution)/shard_map/cond/branch_4_fun/pallas_call | solution.py:208
  53.7 0.6 copy-done.9
  54.5 14.0 %conditional.12 = (bf16[128,256]{1,0:T(8,128)(2,1)S(1)}) conditional(s32[]{:T(128)} %bitcast.4, bf16[128,256]{1,0:T(8,128)(2,1)S(1)} %get-tuple-element.227, bf16[128,256]{1,0:T(8,128)(2,1)S(1)} %get-tuple-element.227, bf16[128,256]{1,0:T(8,128)(2,1)S(1)} %get-tuple-element.227, ...), branch_computations={%region_48.0_spmd, %region_49.0_spmd, %region_50.0_spmd, %region_5... | conditional | bytes 131080 | solution.py:253
  54.6 14.0 %branch_15_fun.6 = bf16[128,256]{1,0:T(8,128)(2,1)S(1)} custom-call(bf16[128,256]{1,0:T(8,128)(2,1)S(1)} %copy.213.rows_ref), custom_call_target="tpu_custom_call" | custom-call | tf_op jit(solution)/shard_map/cond/branch_15_fun/pallas_call | solution.py:208
  68.6 12.7 %conditional.13 = (bf16[512,256]{1,0:T(8,128)(2,1)S(1)}) conditional(s32[]{:T(128)} %bitcast.3, bf16[128,256]{1,0:T(8,128)(2,1)S(1)} %get-tuple-element.240, bf16[128,256]{1,0:T(8,128)(2,1)S(1)} %get-tuple-element.240, bf16[128,256]{1,0:T(8,128)(2,1)S(1)} %get-tuple-element.240, ...), branch_computations={%region_64.0_spmd, %region_65.0_spmd, %region_66.0_spmd, %region_6... | conditional | bytes 8 | solution.py:248
  68.6 12.7 %branch_6_fun.13 = bf16[512,256]{1,0:T(8,128)(2,1)S(1)} custom-call(bf16[128,256]{1,0:T(8,128)(2,1)S(1)} %low_ref.14), custom_call_target="tpu_custom_call" | custom-call | tf_op jit(solution)/shard_map/cond/branch_6_fun/pallas_call | solution.py:93
  81.3 6.0 %shard_map.123 = (f32[512,256]{1,0:T(8,128)}, f32[4,128]{1,0:T(4,128)}, bf16[512,256]{1,0:T(8,128)(2,1)S(1)}) custom-call(s32[1,1,2,64]{3,2,1,0:T(2,128)S(1)} %copy-done.4, s32[1,1,2,64]{3,2,1,0:T(2,128)S(1)} %copy-done.5, s32[1,1,2]{2,1,0:T(1,128)S(1)} %copy-done.7, f32[512,256]{1,0:T(8,128)S(1)} %get-tuple-element.223.src_ref, ...), custom_call_target="tpu_custom_call" | custom-call | tf_op jit(solution)/shard_map/pallas_call | solution.py:343
  87.3 12.5 %conditional.14 = (bf16[128,256]{1,0:T(8,128)(2,1)S(1)}) conditional(s32[]{:T(128)} %bitcast.3, bf16[512,256]{1,0:T(8,128)(2,1)S(1)} %get-tuple-element.233, bf16[512,256]{1,0:T(8,128)(2,1)S(1)} %get-tuple-element.233, bf16[512,256]{1,0:T(8,128)(2,1)S(1)} %get-tuple-element.233, ...), branch_computations={%region_72.0_spmd, %region_73.0_spmd, %region_74.0_spmd, %region_7... | conditional | bytes 8 | solution.py:248
  87.3 12.5 %branch_6_fun.14 = bf16[128,256]{1,0:T(8,128)(2,1)S(1)} custom-call(bf16[512,256]{1,0:T(8,128)(2,1)S(1)} %part_ref.14), custom_call_target="tpu_custom_call" | custom-call | tf_op jit(solution)/shard_map/cond/branch_6_fun/pallas_call | solution.py:175
  99.8 11.3 %conditional.15 = (bf16[128,256]{1,0:T(8,128)(2,1)S(1)}) conditional(s32[]{:T(128)} %bitcast.4, bf16[128,256]{1,0:T(8,128)(2,1)S(1)} %get-tuple-element.242, bf16[128,256]{1,0:T(8,128)(2,1)S(1)} %get-tuple-element.242, bf16[128,256]{1,0:T(8,128)(2,1)S(1)} %get-tuple-element.242, ...), branch_computations={%region_80.0_spmd, %region_81.0_spmd, %region_82.0_spmd, %region_8... | conditional | bytes 131080 | solution.py:253
  99.9 11.3 %branch_15_fun.7 = bf16[128,256]{1,0:T(8,128)(2,1)S(1)} custom-call(bf16[128,256]{1,0:T(8,128)(2,1)S(1)} %copy.228.rows_ref), custom_call_target="tpu_custom_call" | custom-call | tf_op jit(solution)/shard_map/cond/branch_15_fun/pallas_call | solution.py:208
  111.2 0.8 shard_map.124
  (21 shorter events, 0.2 us)
Async XLA Ops:
  0.6 0.7 copy-start.8
  1.3 0.9 copy-start.1
  9.8 21.6 %copy-start = (f32[512,256]{1,0:T(8,128)S(1)}, f32[512,256]{1,0:T(8,128)}, u32[]{:S(2)}) copy-start(f32[512,256]{1,0:T(8,128)} %src_ref.1) | copy-start | bytes 1572868
  9.9 21.6 %copy-start.3 = (f32[64,256]{1,0:T(8,128)S(1)}, f32[64,256]{1,0:T(8,128)}, u32[]{:S(2)}) copy-start(f32[64,256]{1,0:T(8,128)} %rel_ref.3) | copy-start | bytes 196612
  9.9 21.6 %copy-start.5 = (s32[1,1,2,64]{3,2,1,0:T(2,128)S(1)}, s32[1,1,2,64]{3,2,1,0:T(2,128)}, u32[]{:S(2)}) copy-start(s32[1,1,2,64]{3,2,1,0:T(2,128)} %rel_id_ref.3) | copy-start | bytes 1540
  9.9 21.6 %copy-start.6 = (f32[512]{0:T(512)S(1)}, f32[512]{0:T(512)}, u32[]{:S(2)}) copy-start(f32[512]{0:T(512)} %param.106) | copy-start | bytes 6148
  31.4 0.7 copy-start.4
  31.4 0.7 copy-start.7
  49.8 4.0 %copy-start.2 = (f32[128,256]{1,0:T(8,128)S(1)}, f32[128,256]{1,0:T(8,128)}, u32[]{:S(2)}) copy-start(f32[128,256]{1,0:T(8,128)} %table_ref.3) | copy-start | bytes 393220
  53.7 0.7 copy-start.9

commit v3 on v2

--- a/solution.py
+++ b/solution.py
@@ -80,12 +80,14 @@
         passed = part_ref.at[rows(source, chunk)]
         onward.append(copy(12 + chunk, passed, passed, device))
         onward[-1].start()
+    for sent in (*hop.values(), *going_right, *going_left):
+        sent.wait_send()
     for chunk in range(4):
         (going_left if chunk < 2 else going_right)[chunk].wait_recv()
+    for sent in onward:
+        sent.wait_send()
     for passed in onward:
         passed.wait_recv()
-    for sent in (*hop.values(), *going_right, *going_left, *onward):
-        sent.wait_send()
 
 
 def gathered(mask, collective_id, low):
@@ -162,11 +164,11 @@
         if mask:
             back[chunk] = copy(12 + chunk, total.at[rows(0, chunk)], got.at[rows(0, chunk)], to_pair)
             back[chunk].start()
-    for sent in back.values():
-        sent.wait_recv()
     for group in (far_ones, near_ones, added_ones, back):
         for sent in group.values():
             sent.wait_send()
+    for sent in back.values():
+        sent.wait_recv()
 
 
 def reduced(mask, collective_id, dst_part):
@@ -253,39 +255,70 @@
     return lax.switch(index, branches, block)
 
 
-def prepare_kernel(partners_ref, table_ref, low_ref, *index_refs):
-    low_ref[...] = table_ref[...].astype(jnp.bfloat16)
+def prepare_kernel(
+    partners_hbm, table_hbm, state_hbm, low_ref, table_ref, state_ref, *rest
+):
+    *index_refs, partners_ref, done = rest
+    copies = [
+        pltpu.make_async_copy(src, dst, done.at[i])
+        for i, (src, dst) in enumerate(
+            ((partners_hbm, partners_ref), (table_hbm, table_ref), (state_hbm, state_ref))
+        )
+    ]
+    for copy in copies:
+        copy.start()
+    copies[0].wait()
     for round_index in range(ROUNDS):
         mask = partners_ref[round_index, 0]
         index_refs[2 * round_index][0, 0] = (mask >> 5) * 4 + (mask & 3)
         index_refs[2 * round_index + 1][0, 0] = (mask >> 2) & 7
-
-
-def prepared(partners, table):
+    copies[1].wait()
+    low_ref[...] = table_ref[...].astype(jnp.bfloat16)
+    copies[2].wait()
+
+
+def prepared(partners, table, state):
     smem = pl.BlockSpec(memory_space=pltpu.SMEM)
     vmem = pl.BlockSpec(memory_space=pltpu.VMEM)
-    low, *indices = pl.pallas_call(
+    low, table, state, *indices = pl.pallas_call(
         prepare_kernel,
         out_shape=(
             jax.ShapeDtypeStruct(table.shape, jnp.bfloat16),
+            jax.ShapeDtypeStruct(table.shape, jnp.float32),
+            jax.ShapeDtypeStruct(state.shape, jnp.float32),
             *[jax.ShapeDtypeStruct((1, 1), jnp.int32)] * (2 * ROUNDS),
         ),
-        in_specs=[smem, vmem],
-        out_specs=(vmem, *[smem] * (2 * ROUNDS)),
+        in_specs=[pl.BlockSpec(memory_space=pltpu.HBM)] * 3,
+        out_specs=(vmem, vmem, vmem, *[smem] * (2 * ROUNDS)),
+        scratch_shapes=[
+            pltpu.SMEM(partners.shape, jnp.int32),
+            pltpu.SemaphoreType.DMA((3,)),
+        ],
         compiler_params=pltpu.CompilerParams(vmem_limit_bytes=16 * 2**20),
-    )(partners, table)
-    return low, [index[0, 0] for index in indices]
+    )(partners, table, state)
+    return low, table, state, [index[0, 0] for index in indices]
 
 
 UNROLL = 16
 
 
-def tile_kernel(round_index, code_ref, rel_id_ref, count_ref, src_ref, part_ref, rel_ref, state_ref,
-    table_out, state_out, dst_out, src_low, src_grad, dst_grad
+def tile_kernel(
+    round_index, code_hbm, rel_id_hbm, count_hbm, src_ref, part_ref, rel_ref, state_ref,
+    table_out, state_out, dst_out, src_low, src_grad, dst_grad, code_ref, rel_id_ref, count_ref, done
 ):
+    copies = [
+        pltpu.make_async_copy(src, dst, done.at[i])
+        for i, (src, dst) in enumerate(
+            ((code_hbm, code_ref), (rel_id_hbm, rel_id_ref), (count_hbm, count_ref))
+        )
+    ]
+    for copy in copies:
+        copy.start()
     src_low[...] = src_ref[...].astype(jnp.bfloat16).astype(jnp.float32)
     src_grad[...] = jnp.zeros_like(src_grad)
     dst_grad[...] = jnp.zeros_like(dst_grad)
+    for copy in copies:
+        copy.wait()
     live = count_ref[0, 0, round_index]
     row = lax.broadcasted_iota(jnp.int32, (TILE, TILE), 0)
     col = lax.broadcasted_iota(jnp.int32, (TILE, TILE), 1)
@@ -338,7 +371,6 @@
 def tile_work(
     round_index, src_table, src_state, partition, tile_list, rel_list, live_count, rel_table
 ):
-    smem = pl.BlockSpec(memory_space=pltpu.SMEM)
     vmem = pl.BlockSpec(memory_space=pltpu.VMEM)
     return pl.pallas_call(
         functools.partial(tile_kernel, round_index),
@@ -347,12 +379,16 @@
             jax.ShapeDtypeStruct(src_state.shape, jnp.float32),
             jax.ShapeDtypeStruct(partition.shape, jnp.bfloat16),
         ),
-        in_specs=[smem, smem, smem, vmem, vmem, vmem, vmem],
+        in_specs=[pl.BlockSpec(memory_space=pltpu.HBM)] * 3 + [vmem] * 4,
         out_specs=(vmem, vmem, vmem),
         scratch_shapes=[
             pltpu.VMEM(src_table.shape, jnp.float32),
             pltpu.VMEM(src_table.shape, jnp.float32),
             pltpu.VMEM(partition.shape, jnp.float32),
+            pltpu.SMEM(tile_list.shape, jnp.int32),
+            pltpu.SMEM(rel_list.shape, jnp.int32),
+            pltpu.SMEM(live_count.shape, jnp.int32),
+            pltpu.SemaphoreType.DMA((3,)),
         ],
         compiler_params=pltpu.CompilerParams(vmem_limit_bytes=32 * 2**20),
     )(tile_list, rel_list, live_count, src_table, partition, rel_table, src_state)
@@ -363,7 +399,7 @@
 ):
     src_state = src_state.reshape(-1, TILE)
     dst_state = dst_state.reshape(-1, TILE)
-    low, indices = prepared(partners, dst_table)
+    low, dst_table, dst_state, indices = prepared(partners, dst_table, dst_state)
     for round_index in range(ROUNDS):
         others, y = indices[2 * round_index : 2 * round_index + 2]
         moved = along_others(others, low)

time: 112 us -> 105 us (0.938)
  the two profiles are of different devices: /device:TPU:17 before, /device:TPU:1 now
where the time goes in v3:
time: 105 us; the launch traced here: 103 us
  Pallas kernels  97.3 us (93%)
  between operations  3.42 us (3%)
  local copies, waits for them, and re-layouts  2.25 us (2%)
    pallas_call x4, Pallas kernels, permuted(): pl.pallas_call(functools.partial(permute_kernel, mask), out_shape=jax.Sha...  33.7 us
    pallas_call x2, Pallas kernels, gathered(): pl.pallas_call(functools.partial(gather_kernel, mask), out_shape=jax.Shap...  33.2 us
    pallas_call x2, Pallas kernels, reduced(): pl.pallas_call(functools.partial(reduce_kernel, mask), out_shape=jax.Shap...  23.6 us
    pallas_call x2, Pallas kernels, tile_work(): pl.pallas_call(functools.partial(tile_kernel, round_index), out_shape=(ja...  4.74 us
    unnamed x18, local copies, waits for them, and re-layouts  2.22 us

profile of v3, /device:TPU:1, one launch (start us, length us, event | category | flops | bytes accessed | tf_op | source)
XLA Modules:
  0.0 103.4 jit_solution(11860494098594748775)
XLA Ops:
  0.7 0.7 copy-done.7
  1.3 0.9 copy-done.2
  2.2 1.1 %shard_map.120 = (bf16[128,256]{1,0:T(8,128)(2,1)S(1)}, f32[128,256]{1,0:T(8,128)S(1)}, f32[1,128]{1,0:T(1,128)S(1)}, s32[1,1]{1,0:T(1,128)}, s32[1,1]{1,0:T(1,128)}, /*index=5*/s32[1,1]{1,0:T(1,128)}, s32[1,1]{1,0:T(1,128)}) custom-call(s32[2,128]{1,0:T(2,128)S(1)} %copy-done.7, f32[128,256]{1,0:T(8,128)S(1)} %copy-done.2, f32[1,128]{1,0:T(1,128)S(1)} %bitcast.9), custom_call_target="tpu_custom_call" | custom-call | tf_op jit(solution)/shard_map/pallas_call | solution.py:283
  6.0 6.2 %conditional.8 = (bf16[128,256]{1,0:T(8,128)(2,1)S(1)}) conditional(s32[]{:T(128)} %bitcast.2, bf16[128,256]{1,0:T(8,128)(2,1)S(1)} %get-tuple-element.224, bf16[128,256]{1,0:T(8,128)(2,1)S(1)} %get-tuple-element.224, bf16[128,256]{1,0:T(8,128)(2,1)S(1)} %get-tuple-element.224, ...), branch_computations={%region_0.0_spmd, %region_1.0_spmd, %region_2.0_spmd, %region_3.0_... | conditional | bytes 131080 | solution.py:255
  6.0 6.2 %branch_3_fun.8 = bf16[128,256]{1,0:T(8,128)(2,1)S(1)} custom-call(bf16[128,256]{1,0:T(8,128)(2,1)S(1)} %copy.171.rows_ref), custom_call_target="tpu_custom_call" | custom-call | tf_op jit(solution)/shard_map/cond/branch_3_fun/pallas_call | solution.py:210
  12.3 19.4 %conditional.9 = (bf16[512,256]{1,0:T(8,128)(2,1)S(1)}) conditional(s32[]{:T(128)} %bitcast.1, bf16[128,256]{1,0:T(8,128)(2,1)S(1)} %get-tuple-element.240, bf16[128,256]{1,0:T(8,128)(2,1)S(1)} %get-tuple-element.240, bf16[128,256]{1,0:T(8,128)(2,1)S(1)} %get-tuple-element.240, ...), branch_computations={%region_16.0_spmd, %region_17.0_spmd, %region_18.0_spmd, %region_1... | conditional | bytes 8 | solution.py:250
  12.3 19.4 %branch_2_fun.9 = bf16[512,256]{1,0:T(8,128)(2,1)S(1)} custom-call(bf16[128,256]{1,0:T(8,128)(2,1)S(1)} %low_ref.2), custom_call_target="tpu_custom_call" | custom-call | tf_op jit(solution)/shard_map/cond/branch_2_fun/pallas_call | solution.py:95
  31.7 0.6 copy-done.3
  32.4 2.0 %shard_map.121 = (f32[512,256]{1,0:T(8,128)S(1)}, f32[4,128]{1,0:T(4,128)S(1)}, bf16[512,256]{1,0:T(8,128)(2,1)S(1)}) custom-call(s32[1,1,2,64]{3,2,1,0:T(2,128)S(1)} %copy-done.3, s32[1,1,2,64]{3,2,1,0:T(2,128)S(1)} %copy-done.4, s32[1,1,2]{2,1,0:T(1,128)S(1)} %copy-done.6, f32[512,256]{1,0:T(8,128)S(1)} %copy-done, ...), custom_call_target="tpu_custom_call" | custom-call | tf_op jit(solution)/shard_map/pallas_call | solution.py:375
  34.4 12.1 %conditional.10 = (bf16[128,256]{1,0:T(8,128)(2,1)S(1)}) conditional(s32[]{:T(128)} %bitcast.1, bf16[512,256]{1,0:T(8,128)(2,1)S(1)} %get-tuple-element.230, bf16[512,256]{1,0:T(8,128)(2,1)S(1)} %get-tuple-element.230, bf16[512,256]{1,0:T(8,128)(2,1)S(1)} %get-tuple-element.230, ...), branch_computations={%region_24.0_spmd, %region_25.0_spmd, %region_26.0_spmd, %region_2... | conditional | bytes 8 | solution.py:250
  34.4 12.1 %branch_2_fun.10 = bf16[128,256]{1,0:T(8,128)(2,1)S(1)} custom-call(bf16[512,256]{1,0:T(8,128)(2,1)S(1)} %part_ref.2), custom_call_target="tpu_custom_call" | custom-call | tf_op jit(solution)/shard_map/cond/branch_2_fun/pallas_call | solution.py:177
  46.5 11.1 %conditional.11 = (bf16[128,256]{1,0:T(8,128)(2,1)S(1)}) conditional(s32[]{:T(128)} %bitcast.2, bf16[128,256]{1,0:T(8,128)(2,1)S(1)} %get-tuple-element.242, bf16[128,256]{1,0:T(8,128)(2,1)S(1)} %get-tuple-element.242, bf16[128,256]{1,0:T(8,128)(2,1)S(1)} %get-tuple-element.242, ...), branch_computations={%region_32.0_spmd, %region_33.0_spmd, %region_34.0_spmd, %region_3... | conditional | bytes 131080 | solution.py:255
  46.6 11.0 %branch_3_fun.11 = bf16[128,256]{1,0:T(8,128)(2,1)S(1)} custom-call(bf16[128,256]{1,0:T(8,128)(2,1)S(1)} %copy.186.rows_ref), custom_call_target="tpu_custom_call" | custom-call | tf_op jit(solution)/shard_map/cond/branch_3_fun/pallas_call | solution.py:210
  57.6 0.1 shard_map.122
  57.8 4.6 %conditional.12 = (bf16[128,256]{1,0:T(8,128)(2,1)S(1)}) conditional(s32[]{:T(128)} %bitcast.5, bf16[128,256]{1,0:T(8,128)(2,1)S(1)} %get-tuple-element.231, bf16[128,256]{1,0:T(8,128)(2,1)S(1)} %get-tuple-element.231, bf16[128,256]{1,0:T(8,128)(2,1)S(1)} %get-tuple-element.231, ...), branch_computations={%region_48.0_spmd, %region_49.0_spmd, %region_50.0_spmd, %region_5... | conditional | bytes 131080 | solution.py:255
  57.8 4.5 %branch_3_fun.12 = bf16[128,256]{1,0:T(8,128)(2,1)S(1)} custom-call(bf16[128,256]{1,0:T(8,128)(2,1)S(1)} %copy.201.rows_ref), custom_call_target="tpu_custom_call" | custom-call | tf_op jit(solution)/shard_map/cond/branch_3_fun/pallas_call | solution.py:210
  62.4 13.9 %conditional.13 = (bf16[512,256]{1,0:T(8,128)(2,1)S(1)}) conditional(s32[]{:T(128)} %bitcast.4, bf16[128,256]{1,0:T(8,128)(2,1)S(1)} %get-tuple-element.244, bf16[128,256]{1,0:T(8,128)(2,1)S(1)} %get-tuple-element.244, bf16[128,256]{1,0:T(8,128)(2,1)S(1)} %get-tuple-element.244, ...), branch_computations={%region_64.0_spmd, %region_65.0_spmd, %region_66.0_spmd, %region_6... | conditional | bytes 8 | solution.py:250
  62.4 13.8 %branch_1_fun.13 = bf16[512,256]{1,0:T(8,128)(2,1)S(1)} custom-call(bf16[128,256]{1,0:T(8,128)(2,1)S(1)} %low_ref.9), custom_call_target="tpu_custom_call" | custom-call | tf_op jit(solution)/shard_map/cond/branch_1_fun/pallas_call | solution.py:95
  76.3 2.8 %shard_map.123 = (f32[512,256]{1,0:T(8,128)}, f32[4,128]{1,0:T(4,128)}, bf16[512,256]{1,0:T(8,128)(2,1)S(1)}) custom-call(s32[1,1,2,64]{3,2,1,0:T(2,128)S(1)} %copy-done.3, s32[1,1,2,64]{3,2,1,0:T(2,128)S(1)} %copy-done.4, s32[1,1,2]{2,1,0:T(1,128)S(1)} %copy-done.6, f32[512,256]{1,0:T(8,128)S(1)} %get-tuple-element.225.src_ref, ...), custom_call_target="tpu_custom_call" | custom-call | tf_op jit(solution)/shard_map/pallas_call | solution.py:375
  79.0 11.5 %conditional.14 = (bf16[128,256]{1,0:T(8,128)(2,1)S(1)}) conditional(s32[]{:T(128)} %bitcast.4, bf16[512,256]{1,0:T(8,128)(2,1)S(1)} %get-tuple-element.237, bf16[512,256]{1,0:T(8,128)(2,1)S(1)} %get-tuple-element.237, bf16[512,256]{1,0:T(8,128)(2,1)S(1)} %get-tuple-element.237, ...), branch_computations={%region_72.0_spmd, %region_73.0_spmd, %region_74.0_spmd, %region_7... | conditional | bytes 8 | solution.py:250
  79.1 11.5 %branch_1_fun.14 = bf16[128,256]{1,0:T(8,128)(2,1)S(1)} custom-call(bf16[512,256]{1,0:T(8,128)(2,1)S(1)} %part_ref.9), custom_call_target="tpu_custom_call" | custom-call | tf_op jit(solution)/shard_map/cond/branch_1_fun/pallas_call | solution.py:177
  90.6 12.0 %conditional.15 = (bf16[128,256]{1,0:T(8,128)(2,1)S(1)}) conditional(s32[]{:T(128)} %bitcast.5, bf16[128,256]{1,0:T(8,128)(2,1)S(1)} %get-tuple-element.246, bf16[128,256]{1,0:T(8,128)(2,1)S(1)} %get-tuple-element.246, bf16[128,256]{1,0:T(8,128)(2,1)S(1)} %get-tuple-element.246, ...), branch_computations={%region_80.0_spmd, %region_81.0_spmd, %region_82.0_spmd, %region_8... | conditional | bytes 131080 | solution.py:255
  90.6 11.9 %branch_3_fun.15 = bf16[128,256]{1,0:T(8,128)(2,1)S(1)} custom-call(bf16[128,256]{1,0:T(8,128)(2,1)S(1)} %copy.216.rows_ref), custom_call_target="tpu_custom_call" | custom-call | tf_op jit(solution)/shard_map/cond/branch_3_fun/pallas_call | solution.py:210
  102.6 0.8 shard_map.124
  (19 shorter events, 0.1 us)
Async XLA Ops:
  0.6 0.7 copy-start.7
  0.6 0.7 copy-start.8
  1.3 0.9 copy-start.2
  12.2 19.5 %copy-start = (f32[512,256]{1,0:T(8,128)S(1)}, f32[512,256]{1,0:T(8,128)}, u32[]{:S(2)}) copy-start(f32[512,256]{1,0:T(8,128)} %src_ref.1) | copy-start | bytes 1572868
  12.2 19.5 %copy-start.1 = (f32[64,256]{1,0:T(8,128)S(1)}, f32[64,256]{1,0:T(8,128)}, u32[]{:S(2)}) copy-start(f32[64,256]{1,0:T(8,128)} %rel_ref.3) | copy-start | bytes 196612
  12.2 19.5 %copy-start.4 = (s32[1,1,2,64]{3,2,1,0:T(2,128)S(1)}, s32[1,1,2,64]{3,2,1,0:T(2,128)}, u32[]{:S(2)}) copy-start(s32[1,1,2,64]{3,2,1,0:T(2,128)} %rel_id_hbm.3) | copy-start | bytes 1540
  12.2 19.5 %copy-start.5 = (f32[512]{0:T(512)S(1)}, f32[512]{0:T(512)}, u32[]{:S(2)}) copy-start(f32[512]{0:T(512)} %param.106) | copy-start | bytes 6148
  31.7 0.7 copy-start.3
  31.7 0.7 copy-start.6
